TPU v7x, 128 devices: a whole 4x4x4 slice. The times are simulated.
128 devices in a mesh: cfg: 2 (over core), seq: 16 (over z, y), batch: 4 (over x).
Axes of the slice: x: 4, y: 4, z: 4, core: 2. Of those that a mesh axis runs over, the one named last changes fastest.
Arguments:
- queries: bfloat16 [2, 49152, 2048], P('cfg', ('batch', 'seq')), parts along dimension 1, may hold values from -6 to 6
- keys: bfloat16 [2, 49152, 2048], P('cfg', ('batch', 'seq')), parts along dimension 1, may hold values from -6 to 6
- values: bfloat16 [2, 49152, 2048], P('cfg', ('batch', 'seq')), parts along dimension 1, may hold values from -6 to 6
- neighbours: int32 [768, 11], P('batch'), parts along dimension 0, may hold values from 0 to 191, as said below
- w_out: bfloat16 [2048, 4096], replicated, may hold values from -0.125 to 0.125
Outputs:
- guided: bfloat16 [49152, 4096], P(('batch', 'seq'), 'cfg'), parts along dimension 0
There are 4 independent parts, one for each index of `batch`. A program takes and returns all parts, laid end to end along the dimension named above; an argument that names none is the same for every part. Nothing has to cross between parts.
Inputs may be any that keep to these rules, and one draw needn't show every extreme that they name: `neighbours`: row t lists tile t itself first, then tiles of the same camera around it, then one tile of each of the two cameras beside it on the camera cycle.
All inputs are finite; a program needn't handle non-finite values.
Results may differ from a plain program's by a relative error of at most 0.0058.
Values may be sent and summed in bfloat16 or wider, within the bound.
A program may use at most 192 MiB of HBM per device.

v0:
```python
import jax
import jax.numpy as jnp
from jax import lax
from jax.sharding import PartitionSpec as P

HEADS = 16
HD = 128
TILE = 64


guidance_scale = 5.0


def on_device(queries, keys, values, neighbours, w_out):
    tok_rows = queries.shape[1]
    seq_count = lax.axis_size("seq")
    group_heads = HEADS // seq_count
    q_local = queries[0].reshape(tok_rows, seq_count, group_heads, HD)
    k_local = keys[0].reshape(tok_rows, seq_count, group_heads, HD)
    v_local = values[0].reshape(tok_rows, seq_count, group_heads, HD)
    q_heads = lax.all_to_all(q_local, "seq", split_axis=1, concat_axis=0, tiled=True)[:, 0]
    k_heads = lax.all_to_all(k_local, "seq", split_axis=1, concat_axis=0, tiled=True)[:, 0]
    v_heads = lax.all_to_all(v_local, "seq", split_axis=1, concat_axis=0, tiled=True)[:, 0]
    head_count = q_heads.shape[1]
    tile_count = q_heads.shape[0] // TILE
    q_blocks = q_heads.reshape(tile_count // 8, 8, TILE, head_count, HD)
    k_tiles = k_heads.reshape(tile_count, TILE, head_count, HD)
    v_tiles = v_heads.reshape(tile_count, TILE, head_count, HD)
    id_blocks = neighbours.reshape(tile_count // 8, 8, neighbours.shape[1])

    def attend_block(inputs):
        q_block, tile_ids = inputs
        k_near = k_tiles[tile_ids].reshape(8, -1, head_count, HD)
        v_near = v_tiles[tile_ids].reshape(8, -1, head_count, HD)
        scores = jnp.einsum(
            "bqhd,bkhd->bhqk", q_block, k_near, preferred_element_type=jnp.float32
        ) * (1.0 / HD**0.5)
        peak = jnp.max(scores, axis=-1, keepdims=True)
        expval = jnp.exp(scores - peak)
        weights = (expval / jnp.sum(expval, axis=-1, keepdims=True)).astype(jnp.bfloat16)
        result = jnp.einsum("bhqk,bkhd->bqhd", weights, v_near, preferred_element_type=jnp.float32)
        return result.astype(jnp.bfloat16)

    attended_blocks = lax.map(attend_block, (q_blocks, id_blocks))
    attended_rows = attended_blocks.reshape(
        seq_count, tile_count * TILE // seq_count, head_count, HD
    )
    by_source = lax.all_to_all(attended_rows, "seq", split_axis=0, concat_axis=0, tiled=True)
    attended = jnp.transpose(by_source, (1, 0, 2, 3)).reshape(tok_rows, HEADS * HD)
    branch_index = lax.axis_index("cfg")
    half_width = w_out.shape[1] // 2
    projected = jnp.dot(attended, w_out, preferred_element_type=jnp.float32)
    branches = lax.all_gather(projected[None], "cfg", axis=0, tiled=True)
    combined = branches[1] + guidance_scale * (branches[0] - branches[1])
    own_cols = lax.dynamic_slice_in_dim(combined, branch_index * half_width, half_width, 1)
    return own_cols.astype(jnp.bfloat16)


def solution(mesh):
    return jax.shard_map(
        on_device,
        mesh=mesh,
        in_specs=(
            P("cfg", ("batch", "seq"), None),
            P("cfg", ("batch", "seq"), None),
            P("cfg", ("batch", "seq"), None),
            P("batch", None),
            P(),
        ),
        out_specs=P(("batch", "seq"), "cfg"),
        check_vma=False,
    )
```

profile of v0, /device:TPU:1, one launch (start us, length us, event | category | flops | bytes accessed | tf_op | source)
XLA Modules:
  0.0 610.2 jit_solution(13629499313454375515)
XLA Ops:
  6.5 4.6 copy.30
  11.2 8.6 %all-to-all-start = ((bf16[768,16,1,128]{0,3,2,1:T(8,128)(2,1)}), bf16[768,16,1,128]{0,3,2,1:T(8,128)(2,1)S(1)}, u32[]{:S(2)}, u32[]{:S(2)}) async-start(bf16[768,16,1,128]{0,3,2,1:T(8,128)(2,1)} %bitcast.88), calls=%async_computation | async-start | bytes 6291456 | tf_op jit(solution)/shard_map/all_to_all | solution.py:23
  19.8 4.7 copy.35
  24.4 42.0 %all-to-all-done = bf16[768,16,1,128]{0,3,2,1:T(8,128)(2,1)S(1)} async-done(((bf16[768,16,1,128]{0,3,2,1:T(8,128)(2,1)}), bf16[768,16,1,128]{0,3,2,1:T(8,128)(2,1)S(1)}, u32[]{:S(2)}, u32[]{:S(2)}) %all-to-all-start) | async-done | bytes 3145760 | tf_op jit(solution)/shard_map/all_to_all | solution.py:23
  66.4 4.5 all-to-all-start.2
  70.9 4.6 copy.33
  75.5 4.7 copy.34
  80.2 34.4 %all-to-all-done.2 = bf16[768,16,1,128]{0,3,2,1:T(8,128)(2,1)} async-done(((bf16[768,16,1,128]{0,3,2,1:T(8,128)(2,1)}), bf16[768,16,1,128]{0,3,2,1:T(8,128)(2,1)}, u32[]{:S(2)}, u32[]{:S(2)}) %all-to-all-start.2) | async-done | bytes 3145760 | tf_op jit(solution)/shard_map/all_to_all | solution.py:22
  114.6 4.5 all-to-all-start.1
  122.0 4.7 copy.37
  126.8 32.1 %all-to-all-done.1 = bf16[768,16,1,128]{3,0,2,1:T(8,128)(2,1)} async-done(((bf16[768,16,1,128]{3,0,2,1:T(8,128)(2,1)}), bf16[768,16,1,128]{3,0,2,1:T(8,128)(2,1)}, u32[]{:S(2)}, u32[]{:S(2)}) %all-to-all-start.1) | async-done | bytes 3145760 | tf_op jit(solution)/shard_map/all_to_all | solution.py:21
  158.9 313.3 %while.10 = (s32[]{:T(128)}, bf16[24,8,64,1,128]{4,2,1,3,0:T(8,128)(2,1)}, s32[24,8,11]{2,1,0:T(8,128)S(1)}, bf16[192,64,1,128]{3,1,0,2:T(8,128)(2,1)}, bf16[24,...) while((s32[]{:T(128)}, bf16[24,8,64,1,128]{4,2,1,3,0:T(8,128)(2,1)}, ...), condition=%wide.region_3.4_spmd, body=%wide.region_0.3_spmd.sunk | while | flops 279415936 | bytes 15086085 | solution.py:44
  159.0 3.8 gather_fusion
  168.8 3.1 fusion.43
  172.0 3.8 gather_fusion
  181.9 3.1 fusion.43
  185.1 3.8 gather_fusion
  198.1 3.8 gather_fusion
  211.2 3.8 gather_fusion
  221.1 3.1 fusion.43
  224.2 3.8 gather_fusion
  237.3 3.8 gather_fusion
  247.2 3.1 fusion.43
  250.3 3.8 gather_fusion
  263.4 3.8 gather_fusion
  273.3 3.1 fusion.43
  276.4 3.8 gather_fusion
  289.5 3.8 gather_fusion
  302.5 3.8 gather_fusion
  312.4 3.1 fusion.43
  315.6 3.8 gather_fusion
  328.6 3.8 gather_fusion
  338.5 3.1 fusion.43
  341.7 3.8 gather_fusion
  354.8 3.8 gather_fusion
  367.8 3.8 gather_fusion
  380.9 3.8 gather_fusion
  393.9 3.8 gather_fusion
  407.0 3.8 gather_fusion
  420.0 3.8 gather_fusion
  433.1 3.8 gather_fusion
  446.1 3.8 gather_fusion
  459.2 3.8 gather_fusion
  472.1 45.4 %all_to_all.50 = bf16[16,768,1,128]{3,1,2,0:T(8,128)(2,1)S(1)} all-to-all(bf16[16,768,1,128]{3,1,2,0:T(8,128)(2,1)} %bitcast.90), channel_id=1, replica_groups=mesh['cfg'=2,'seq'=16,'batch'=4] {'seq'}, dimensions={0} | all-to-all | bytes 6291456 | tf_op jit(solution)/shard_map/all_to_all | solution.py:48
  520.2 20.4 %fusion.21 = f32[768,4096]{1,0:T(8,128)} fusion(bf16[768,2048]{0,1:T(8,128)(2,1)} %bitcast.91, bf16[2048,4096]{1,0:T(8,128)(2,1)} %param.11), kind=kOutput, calls=%fused_computation.24 | convolution fusion | flops 12884901888 | bytes 32505856 | tf_op jit(solution)/shard_map/dot_general | solution.py:52
  540.7 42.5 %all-gather.3.cloned.1.call-done = f32[1536,4096]{1,0:T(8,128)} async-done(((f32[768,4096]{1,0:T(8,128)}), f32[1536,4096]{1,0:T(8,128)}) %all-gather.3.cloned.1.call-update) | async-done | bytes 25165840 | tf_op jit(solution)/shard_map/all_gather | solution.py:53
  583.2 14.2 %fusion.20 = (f32[768,4096]{1,0:T(8,128)S(1)}, f32[768,4096]{1,0:T(8,128)}) fusion(f32[1536,4096]{1,0:T(8,128)} %all-gather.3.cloned.1.call-done), kind=kLoop, calls=%fused_computation.23 | loop fusion | bytes 50331648 | tf_op jit(solution)/shard_map/slice | solution.py:54
  597.3 6.0 fusion.16
  (169 shorter events, 205.8 us)
Async XLA Ops:
  11.2 55.2 %all-to-all-start = ((bf16[768,16,1,128]{0,3,2,1:T(8,128)(2,1)}), bf16[768,16,1,128]{0,3,2,1:T(8,128)(2,1)S(1)}, u32[]{:S(2)}, u32[]{:S(2)}) async-start(bf16[768,16,1,128]{0,3,2,1:T(8,128)(2,1)} %bitcast.88), calls=%async_computation | async-start | bytes 6291456 | tf_op jit(solution)/shard_map/all_to_all | solution.py:23
  66.4 48.2 %all-to-all-start.2 = ((bf16[768,16,1,128]{0,3,2,1:T(8,128)(2,1)}), bf16[768,16,1,128]{0,3,2,1:T(8,128)(2,1)}, u32[]{:S(2)}, u32[]{:S(2)}) async-start(bf16[768,16,1,128]{0,3,2,1:T(8,128)(2,1)} %bitcast.87), calls=%async_computation.2 | async-start | bytes 6291456 | tf_op jit(solution)/shard_map/all_to_all | solution.py:22
  80.2 38.9 %copy-start = (s32[192,11]{0,1:T(8,128)S(1)}, s32[192,11]{0,1:T(8,128)}, u32[]{:S(2)}) copy-start(s32[192,11]{0,1:T(8,128)} %param.10) | copy-start | bytes 25348
  114.6 44.3 %all-to-all-start.1 = ((bf16[768,16,1,128]{3,0,2,1:T(8,128)(2,1)}), bf16[768,16,1,128]{3,0,2,1:T(8,128)(2,1)}, u32[]{:S(2)}, u32[]{:S(2)}) async-start(bf16[768,16,1,128]{3,0,2,1:T(8,128)(2,1)} %copy.34), calls=%async_computation.1 | async-start | bytes 6291456 | tf_op jit(solution)/shard_map/all_to_all | solution.py:21
  119.1 464.1 %all-gather.3.cloned.1.call-start = ((), (), s32[]{:S(2)}) async-start(), calls=%async_computation.4 | async-start | bytes 37748736 | tf_op jit(solution)/shard_map/all_gather | solution.py:53
Sparse Core Ops, SparseCore 0:
  540.8 42.3 all-gather.2
where the time goes:
time: 614 us; the launch traced here: 610 us
  local copies, waits for them, and re-layouts  201 us (33%)
  matrix products  175 us (29%)
  waiting for transfers between devices  151 us (25%)
  blocking collectives  45.4 us (7%)
  starting transfers between devices  17.6 us (3%)
  between operations  13.5 us (2%)
  other arithmetic  6.31 us (1%)
    gather x24, local copies, waits for them, and re-layouts, attend_block(): v_near = v_tiles[tile_ids].reshape(8, -1, head_count, HD)  91.2 us
    dot_general x24, matrix products, attend_block(): jnp.einsum('bhqk,bkhd->bqhd', weights, v_near, preferred_element_type=jnp...  73.9 us
    gather x24, local copies, waits for them, and re-layouts, attend_block(): k_near = k_tiles[tile_ids].reshape(8, -1, head_count, HD)  65.1 us
    all_to_all x1, blocking collectives, on_device(): lax.all_to_all(attended_rows, 'seq', split_axis=0, concat_axis=0, tiled=T...  45.4 us
    sub x24, matrix products, attend_block(): expval = jnp.exp(scores - peak)  42.8 us
    all_gather x1, waiting for transfers between devices, on_device(): branches = lax.all_gather(projected[None], 'cfg', axis=0, tiled=True)  42.5 us
    all_to_all x1, waiting for transfers between devices, on_device(): lax.all_to_all(v_local, 'seq', split_axis=1, concat_axis=0, tiled=True)  42 us
    dot_general x24, matrix products, attend_block(): jnp.einsum('bqhd,bkhd->bhqk', q_block, k_near, preferred_element_type=jnp...  37.6 us
  transfers between devices with their start and end apart: 4, of which 4 were waited for; matrix products, arithmetic and copies ran while one was open for 4% of the time, Pallas kernels for 0%

commit v1 on v0

v1 whole, which is shorter than its diff:
```python
import jax
import jax.numpy as jnp
import numpy as np
from jax import lax
from jax.experimental import pallas as pl
from jax.experimental.pallas import tpu as pltpu
from jax.sharding import PartitionSpec as P

HEADS = 16
HD = 128
TILE = 64
GUIDANCE = 5.0
MESH = pl.DeviceIdType.MESH

SEQ = 16
RING = 4
NB = 11
ROWS = 768
ROUNDS = 6
TILES = ROWS // TILE
PAIR = 2 * TILE
PAIRS = ROUNDS * SEQ
SPAN = NB * TILE
EXP_SCALE = float(np.log2(np.e) / HD**0.5)

OFFSETS = (
    (0, 1), (0, 3), (1, 0), (3, 0),
    (1, 1), (3, 3), (1, 3), (3, 1),
    (0, 2), (2, 0),
    (1, 2), (3, 2), (2, 1), (2, 3),
    (2, 2),
)


def kernel(
    ids, q_hbm, k_hbm, v_hbm, w_hbm, out_hbm,
    q_buf, k_buf, v_buf, w_buf, att, swapped, folded, gathered, out_buf,
    s_even, s_odd, p_even, p_odd,
    w_sem, out_sem, k_send, k_recv, v_send, v_recv, q_send, q_recv,
    x_send, x_recv, g_send, g_recv, f_send, f_recv,
):
    core = lax.axis_index("cfg")
    me = lax.axis_index("seq")
    z, y = me // RING, me % RING
    other_core = {"cfg": 1 - core}
    peers = [lax.rem(z + dz, RING) * RING + lax.rem(y + dy, RING) for dz, dy in OFFSETS]

    def await_bytes(ref, sem):
        pltpu.make_async_copy(ref, ref, sem).wait()

    barrier = pltpu.get_barrier_semaphore()
    for peer in peers:
        pl.semaphore_signal(barrier, inc=1, device_id={"seq": peer}, device_id_type=MESH)
    pl.semaphore_signal(barrier, inc=1, device_id=other_core, device_id_type=MESH)
    pl.semaphore_wait(barrier, SEQ)

    def head_cols(head):
        return pl.ds(pl.multiple_of(head * HD, HD), HD)

    def scatter(src, buf, send, recv):
        tiles = pl.ds(me * TILES, TILES)
        for peer in peers:
            pltpu.make_async_remote_copy(
                src_ref=src.at[0, :, :, head_cols(peer)],
                dst_ref=buf.at[tiles],
                send_sem=send,
                recv_sem=recv,
                device_id={"seq": peer},
                device_id_type=MESH,
            ).start()
        pltpu.make_async_copy(src.at[0, :, :, head_cols(me)], buf.at[tiles], recv).start()

    def scatter_queries(r, _):
        rows = pl.ds(pl.multiple_of(r * PAIR, PAIR), PAIR)
        for peer in peers:
            pltpu.make_async_remote_copy(
                src_ref=q_hbm.at[0, rows, head_cols(peer)],
                dst_ref=q_buf.at[r, me],
                send_sem=q_send,
                recv_sem=q_recv.at[r],
                device_id={"seq": peer},
                device_id_type=MESH,
            ).start()
        pltpu.make_async_copy(
            q_hbm.at[0, rows, head_cols(me)], q_buf.at[r, me], q_recv.at[r]
        ).start()
        return 0

    remote_tiles = pl.ds(0, (SEQ - 1) * TILES)
    scatter(k_hbm, k_buf, k_send, k_recv)
    half_cols = w_hbm.shape[1] // 2
    w_copy = pltpu.make_async_copy(
        w_hbm.at[:, pl.ds(pl.multiple_of(core * half_cols, half_cols), half_cols)], w_buf, w_sem
    )
    w_copy.start()
    for ref in (s_even, s_odd, p_even, p_odd):
        ref[...] = jnp.zeros_like(ref)
    await_bytes(k_buf.at[remote_tiles], k_send)
    scatter(v_hbm, v_buf, v_send, v_recv)
    await_bytes(v_buf.at[remote_tiles], v_send)
    lax.fori_loop(0, ROUNDS, scatter_queries, 0)
    await_bytes(k_buf, k_recv)
    await_bytes(v_buf, v_recv)
    w_copy.wait()

    def near(buf, tile):
        return jnp.concatenate([buf[ids[tile, j]] for j in range(NB)], axis=0)

    def near_pair(buf, pair):
        tile = (pair % SEQ) * TILES + (pair // SEQ) * 2
        return jnp.concatenate([near(buf, tile), near(buf, tile + 1)], axis=1)

    def step(i, scores_in, scores_out, probs_in, probs_out):
        done = jnp.maximum(i - 2, 0)
        result = lax.dot_general(
            probs_in[...], near_pair(v_buf, done), (((0,), (0,)), ((), ())),
            preferred_element_type=jnp.float32,
        )
        att[done // SEQ, 0, done % SEQ] = result[:TILE, :HD].astype(jnp.bfloat16)
        att[done // SEQ, 1, done % SEQ] = result[TILE:, HD:].astype(jnp.bfloat16)
        scores = scores_in[...]
        peak = jnp.max(scores, axis=0, keepdims=True) * EXP_SCALE
        expval = jnp.exp2(scores * EXP_SCALE - peak)
        total = jnp.sum(expval, axis=0, keepdims=True)
        probs_out[...] = (expval * (1.0 / total)).astype(jnp.bfloat16)
        pair = jnp.minimum(i, PAIRS - 1)
        queries = q_buf[pair // SEQ, pair % SEQ]
        zero = jnp.zeros((TILE, HD), jnp.bfloat16)
        blocks = jnp.concatenate(
            [
                jnp.concatenate([queries[:TILE], zero], axis=1),
                jnp.concatenate([zero, queries[TILE:]], axis=1),
            ],
            axis=0,
        )
        scores_out[...] = lax.dot_general(
            near_pair(k_buf, pair), blocks, (((1,), (1,)), ((), ())),
            preferred_element_type=jnp.float32,
        )

    def steps(first, count):
        def two(n, _):
            i = first + 2 * n
            step(i, s_odd, s_even, p_even, p_odd)
            step(i + 1, s_even, s_odd, p_odd, p_even)
            return 0

        lax.fori_loop(0, count // 2, two, 0)

    def swap(r):
        return pltpu.make_async_remote_copy(
            src_ref=att.at[r, 1 - core],
            dst_ref=swapped.at[r],
            send_sem=x_send,
            recv_sem=x_recv.at[r],
            device_id=other_core,
            device_id_type=MESH,
        )

    own_gain = jnp.where(core == 0, GUIDANCE, 1.0 - GUIDANCE).astype(jnp.float32)
    other_gain = 1.0 - own_gain

    def round_rows(r, half):
        return pl.ds(pl.multiple_of(r * PAIR + half * TILE, TILE), TILE)

    def fold(r):
        await_bytes(swapped.at[r], x_recv.at[r])

        def some(n, _):
            part = pl.ds(n * 4, 4)
            own = att[r, core, part].astype(jnp.float32)
            other = swapped[r, part].astype(jnp.float32)
            folded[r, part] = (own * own_gain + other * other_gain).astype(jnp.bfloat16)
            return 0

        lax.fori_loop(0, SEQ // 4, some, 0)
        rows = round_rows(r, core)
        for peer in peers:
            pltpu.make_async_remote_copy(
                src_ref=folded.at[r, peer],
                dst_ref=gathered.at[rows, head_cols(me)],
                send_sem=g_send,
                recv_sem=g_recv.at[r],
                device_id={"seq": peer},
                device_id_type=MESH,
            ).start()
        pltpu.make_async_copy(
            folded.at[r, me], gathered.at[rows, head_cols(me)], g_recv.at[r]
        ).start()

    def forward(r):
        rows = round_rows(r, core)
        await_bytes(gathered.at[rows], g_recv.at[r])
        pltpu.make_async_remote_copy(
            src_ref=gathered.at[rows],
            dst_ref=gathered.at[rows],
            send_sem=f_send,
            recv_sem=f_recv.at[r],
            device_id=other_core,
            device_id_type=MESH,
        ).start()

    def project(r):
        await_bytes(gathered.at[round_rows(r, 1 - core)], f_recv.at[r])
        rows = pl.ds(pl.multiple_of(r * PAIR, PAIR), PAIR)

        def columns(n, _):
            cols = pl.ds(pl.multiple_of(n * 512, 512), 512)
            out_buf[rows, cols] = jnp.dot(
                gathered[rows, :], w_buf[:, cols], preferred_element_type=jnp.float32
            ).astype(jnp.bfloat16)
            return 0

        lax.fori_loop(0, half_cols // 512, columns, 0)
        pltpu.make_async_copy(out_buf.at[rows], out_hbm.at[rows], out_sem).start()

    def one_round(r, _):
        await_bytes(q_buf.at[r], q_recv.at[r])
        steps(r * SEQ, 2)
        pl.when(r >= 1)(lambda: swap(r - 1).start())
        steps(r * SEQ + 2, 8)
        pl.when(r >= 1)(lambda: fold(r - 1))
        steps(r * SEQ + 10, 6)
        pl.when(r >= 1)(lambda: forward(r - 1))
        pl.when(r >= 2)(lambda: project(r - 2))
        return 0

    lax.fori_loop(0, ROUNDS, one_round, 0)
    steps(PAIRS, 2)
    last = ROUNDS - 1
    swap(last).start()
    project(last - 1)
    fold(last)
    forward(last)
    project(last)

    await_bytes(q_buf.at[:, pl.ds(0, SEQ - 1)], q_send)
    await_bytes(swapped, x_send)
    await_bytes(folded.at[:, pl.ds(0, SEQ - 1)], g_send)
    await_bytes(swapped, f_send)
    await_bytes(out_buf, out_sem)


def by_tile(tokens):
    return tokens.reshape(1, TILES, TILE, HEADS * HD)


def on_device(queries, keys, values, neighbours, w_out):
    bf16, f32 = jnp.bfloat16, jnp.float32
    dma = pltpu.SemaphoreType.DMA
    vmem = pltpu.VMEM
    width = w_out.shape[1] // 2
    return pl.pallas_call(
        kernel,
        out_shape=jax.ShapeDtypeStruct((ROWS, width), bf16),
        in_specs=[pl.BlockSpec(memory_space=pltpu.SMEM)]
        + [pl.BlockSpec(memory_space=pl.ANY)] * 4,
        out_specs=pl.BlockSpec(memory_space=pl.ANY),
        scratch_shapes=[
            vmem((ROUNDS, SEQ, PAIR, HD), bf16),
            vmem((SEQ * TILES, TILE, HD), bf16),
            vmem((SEQ * TILES, TILE, HD), bf16),
            vmem((HEADS * HD, width), bf16),
            vmem((ROUNDS, 2, SEQ, TILE, HD), bf16),
            vmem((ROUNDS, SEQ, TILE, HD), bf16),
            vmem((ROUNDS, SEQ, TILE, HD), bf16),
            vmem((ROWS, HEADS * HD), bf16),
            vmem((ROWS, width), bf16),
            vmem((SPAN, PAIR), f32),
            vmem((SPAN, PAIR), f32),
            vmem((SPAN, PAIR), bf16),
            vmem((SPAN, PAIR), bf16),
            dma, dma,
            dma, dma, dma, dma,
            dma, dma((ROUNDS,)),
            dma, dma((ROUNDS,)),
            dma, dma((ROUNDS,)),
            dma, dma((ROUNDS,)),
        ],
        compiler_params=pltpu.CompilerParams(
            collective_id=0, has_side_effects=True, vmem_limit_bytes=56 * 2**20
        ),
        cost_estimate=pl.CostEstimate(
            flops=11_000_000_000, bytes_accessed=20 * 2**20, transcendentals=8_700_000
        ),
    )(neighbours, queries, by_tile(keys), by_tile(values), w_out)


def solution(mesh):
    return jax.shard_map(
        on_device,
        mesh=mesh,
        in_specs=(
            P("cfg", ("batch", "seq"), None),
            P("cfg", ("batch", "seq"), None),
            P("cfg", ("batch", "seq"), None),
            P("batch", None),
            P(),
        ),
        out_specs=P(("batch", "seq"), "cfg"),
        check_vma=False,
    )
```

time: 614 us -> 190 us (0.31)
  local copies, waits for them, and re-layouts: 201 us -> 5.43 us
  Pallas kernels: 0 us -> 184 us
  matrix products: 175 us -> 0 us
  waiting for transfers between devices: 151 us -> 0 us
  blocking collectives: 45.4 us -> 0 us
  starting transfers between devices: 17.6 us -> 0 us
  between operations: 13.5 us -> 0.01 us
  other arithmetic: 6.31 us -> 0 us
    pallas_call x0 -> x1, Pallas kernels: none -> 184 us  [on_device(): pl.pallas_call(kernel, out_shape=jax.ShapeDtypeStruct((ROWS, width), bf16...]
    gather x48 -> x0, local copies, waits for them, and re-layouts: 156 us -> none  [the longest x24 91.2 us: attend_block(): v_near = v_tiles[tile_ids].reshape(8, -1, head_count, HD)]
    dot_general x49 -> x0, matrix products: 132 us -> none  [the longest x24 73.9 us: attend_block(): jnp.einsum('bhqk,bkhd->bqhd', weights, v_near, preferred_element_type=jnp...]
    all_to_all x3 -> x0, waiting for transfers between devices: 108 us -> none  [the longest x1 42 us: on_device(): lax.all_to_all(v_local, 'seq', split_axis=1, concat_axis=0, tiled=True)]
    all_to_all x1 -> x0, blocking collectives: 45.4 us -> none  [on_device(): lax.all_to_all(attended_rows, 'seq', split_axis=0, concat_axis=0, tiled=T...]
    sub x24 -> x0, matrix products: 42.8 us -> none  [attend_block(): expval = jnp.exp(scores - peak)]
    all_gather x1 -> x0, waiting for transfers between devices: 42.5 us -> none  [on_device(): branches = lax.all_gather(projected[None], 'cfg', axis=0, tiled=True)]
    all_to_all x3 -> x0, starting transfers between devices: 17.6 us -> none  [the longest x1 8.6 us: on_device(): lax.all_to_all(v_local, 'seq', split_axis=1, concat_axis=0, tiled=True)]
  transfers between devices with their start and end apart: 4 -> 0, of which waited for: 4 -> 0; matrix products, arithmetic and copies ran while one was open for 4% -> 0% of each run, Pallas kernels for 0% -> 0%
where the time goes in v1:
time: 190 us; the launch traced here: 189 us
  Pallas kernels  184 us (97%)
  local copies, waits for them, and re-layouts  5.43 us (3%)
    pallas_call x1, Pallas kernels, on_device(): pl.pallas_call(kernel, out_shape=jax.ShapeDtypeStruct((ROWS, width), bf16...  184 us
    unnamed x2, local copies, waits for them, and re-layouts  5.43 us

profile of v1, /device:TPU:1, one launch (start us, length us, event | category | flops | bytes accessed | tf_op | source)
XLA Modules:
  0.0 189.5 jit_solution(1918061910291137954)
XLA Ops:
  0.0 1.5 copy.6.ids
  1.5 184.0 %shard_map.55 = bf16[768,2048]{1,0:T(8,128)(2,1)} custom-call(s32[192,11]{1,0:T(8,128)} %copy.6.ids, bf16[1,768,2048]{2,1,0:T(8,128)(2,1)} %q_hbm.1, bf16[1,12,64,2048]{3,2,1,0:T(8,128)(2,1)} %bitcast.2, bf16[1,12,64,2048]{3,2,1,0:T(8,128)(2,1)} %bitcast.3, bf16[2048,4096]{1,0:T(8,128)(2,1)} %w_hbm.1), custom_call_target="tpu_custom_call" | custom-call | flops 11000000512 | bytes 20971520 | tf_op jit(solution)/shard_map/pallas_call | solution.py:253
  185.5 4.0 %copy.8 = bf16[768,2048]{1,0:T(8,128)(2,1)} copy(bf16[768,2048]{1,0:T(8,128)(2,1)} %shard_map.55) | data formatting | bytes 6291456

commit v2 on v1

--- a/solution.py
+++ b/solution.py
@@ -18,6 +18,7 @@
 ROWS = 768
 ROUNDS = 6
 TILES = ROWS // TILE
+BLK = 2
 PAIR = 2 * TILE
 PAIRS = ROUNDS * SEQ
 SPAN = NB * TILE
@@ -33,10 +34,10 @@
 
 
 def kernel(
-    ids, q_hbm, k_hbm, v_hbm, w_hbm, out_hbm,
-    q_buf, k_buf, v_buf, w_buf, att, swapped, folded, gathered, out_buf,
+    ids_hbm, q_hbm, k_hbm, v_hbm, w_hbm, out_hbm,
+    q_buf, k_buf, v_buf, w_buf, att, swapped, folded, gathered,
     s_even, s_odd, p_even, p_odd,
-    w_sem, out_sem, k_send, k_recv, v_send, v_recv, q_send, q_recv,
+    ids, ids_sem, w_sem, k_send, k_recv, v_send, v_recv, q_send, q_recv,
     x_send, x_recv, g_send, g_recv, f_send, f_recv,
 ):
     core = lax.axis_index("cfg")
@@ -59,15 +60,20 @@
 
     def scatter(src, buf, send, recv):
         tiles = pl.ds(me * TILES, TILES)
-        for peer in peers:
-            pltpu.make_async_remote_copy(
-                src_ref=src.at[0, :, :, head_cols(peer)],
-                dst_ref=buf.at[tiles],
-                send_sem=send,
-                recv_sem=recv,
-                device_id={"seq": peer},
-                device_id_type=MESH,
-            ).start()
+
+        def block(n, _):
+            for peer in peers:
+                pltpu.make_async_remote_copy(
+                    src_ref=src.at[0, pl.ds(n * BLK, BLK), :, head_cols(peer)],
+                    dst_ref=buf.at[pl.ds(me * TILES + n * BLK, BLK)],
+                    send_sem=send,
+                    recv_sem=recv,
+                    device_id={"seq": peer},
+                    device_id_type=MESH,
+                ).start()
+            return 0
+
+        lax.fori_loop(0, TILES // BLK, block, 0)
         pltpu.make_async_copy(src.at[0, :, :, head_cols(me)], buf.at[tiles], recv).start()
 
     def scatter_queries(r, _):
@@ -93,15 +99,18 @@
         w_hbm.at[:, pl.ds(pl.multiple_of(core * half_cols, half_cols), half_cols)], w_buf, w_sem
     )
     w_copy.start()
+    ids_copy = pltpu.make_async_copy(ids_hbm, ids, ids_sem)
+    ids_copy.start()
     for ref in (s_even, s_odd, p_even, p_odd):
         ref[...] = jnp.zeros_like(ref)
+    scatter(v_hbm, v_buf, v_send, v_recv)
+    lax.fori_loop(0, ROUNDS, scatter_queries, 0)
     await_bytes(k_buf.at[remote_tiles], k_send)
-    scatter(v_hbm, v_buf, v_send, v_recv)
     await_bytes(v_buf.at[remote_tiles], v_send)
-    lax.fori_loop(0, ROUNDS, scatter_queries, 0)
     await_bytes(k_buf, k_recv)
     await_bytes(v_buf, v_recv)
     w_copy.wait()
+    ids_copy.wait()
 
     def near(buf, tile):
         return jnp.concatenate([buf[ids[tile, j]] for j in range(NB)], axis=0)
@@ -206,13 +215,12 @@
 
         def columns(n, _):
             cols = pl.ds(pl.multiple_of(n * 512, 512), 512)
-            out_buf[rows, cols] = jnp.dot(
+            out_hbm[rows, cols] = jnp.dot(
                 gathered[rows, :], w_buf[:, cols], preferred_element_type=jnp.float32
             ).astype(jnp.bfloat16)
             return 0
 
         lax.fori_loop(0, half_cols // 512, columns, 0)
-        pltpu.make_async_copy(out_buf.at[rows], out_hbm.at[rows], out_sem).start()
 
     def one_round(r, _):
         await_bytes(q_buf.at[r], q_recv.at[r])
@@ -221,24 +229,27 @@
         steps(r * SEQ + 2, 8)
         pl.when(r >= 1)(lambda: fold(r - 1))
         steps(r * SEQ + 10, 6)
-        pl.when(r >= 1)(lambda: forward(r - 1))
-        pl.when(r >= 2)(lambda: project(r - 2))
         return 0
 
     lax.fori_loop(0, ROUNDS, one_round, 0)
     steps(PAIRS, 2)
     last = ROUNDS - 1
     swap(last).start()
-    project(last - 1)
     fold(last)
-    forward(last)
+    forward(0)
+
+    def finish(r, _):
+        forward(r + 1)
+        project(r)
+        return 0
+
+    lax.fori_loop(0, last, finish, 0)
     project(last)
 
     await_bytes(q_buf.at[:, pl.ds(0, SEQ - 1)], q_send)
     await_bytes(swapped, x_send)
     await_bytes(folded.at[:, pl.ds(0, SEQ - 1)], g_send)
     await_bytes(swapped, f_send)
-    await_bytes(out_buf, out_sem)
 
 
 def by_tile(tokens):
@@ -252,10 +263,9 @@
     width = w_out.shape[1] // 2
     return pl.pallas_call(
         kernel,
-        out_shape=jax.ShapeDtypeStruct((ROWS, width), bf16),
-        in_specs=[pl.BlockSpec(memory_space=pltpu.SMEM)]
-        + [pl.BlockSpec(memory_space=pl.ANY)] * 4,
-        out_specs=pl.BlockSpec(memory_space=pl.ANY),
+        out_shape=pltpu.VMEM((ROWS, width), bf16),
+        in_specs=[pl.BlockSpec(memory_space=pl.ANY)] * 5,
+        out_specs=pl.BlockSpec(memory_space=pltpu.VMEM),
         scratch_shapes=[
             vmem((ROUNDS, SEQ, PAIR, HD), bf16),
             vmem((SEQ * TILES, TILE, HD), bf16),
@@ -265,12 +275,11 @@
             vmem((ROUNDS, SEQ, TILE, HD), bf16),
             vmem((ROUNDS, SEQ, TILE, HD), bf16),
             vmem((ROWS, HEADS * HD), bf16),
-            vmem((ROWS, width), bf16),
             vmem((SPAN, PAIR), f32),
             vmem((SPAN, PAIR), f32),
             vmem((SPAN, PAIR), bf16),
             vmem((SPAN, PAIR), bf16),
-            dma, dma,
+            pltpu.SMEM((SEQ * TILES, NB), jnp.int32), dma, dma,
             dma, dma, dma, dma,
             dma, dma((ROUNDS,)),
             dma, dma((ROUNDS,)),

time: 190 us -> 136 us (0.72)
  Pallas kernels: 184 us -> 133 us
  local copies, waits for them, and re-layouts: 5.43 us -> 3.13 us
    pallas_call x1, Pallas kernels: 184 us -> 133 us  [on_device(): pl.pallas_call(kernel, out_shape=pltpu.VMEM((ROWS, width), bf16), in_spec...]
    unnamed x2, local copies, waits for them, and re-layouts: 5.43 us -> 3.13 us
where the time goes in v2:
time: 136 us
  Pallas kernels  133 us (98%)
  local copies, waits for them, and re-layouts  3.13 us (2%)
    pallas_call x1, Pallas kernels, on_device(): pl.pallas_call(kernel, out_shape=pltpu.VMEM((ROWS, width), bf16), in_spec...  133 us
    unnamed x2, local copies, waits for them, and re-layouts  3.13 us

profile of v2, /device:TPU:1, one launch (start us, length us, event | category | flops | bytes accessed | tf_op | source)
XLA Modules:
  0.0 136.3 jit_solution(14664313707131675862)
XLA Ops:
  0.0 1.5 %copy.6.ids_hbm = s32[192,11]{1,0:T(8,128)} copy(s32[192,11]{0,1:T(8,128)} %param.8) | data formatting | bytes 16896 | tf_op args[3]
  1.5 133.2 %shard_map.55 = bf16[768,2048]{1,0:T(8,128)(2,1)S(1)} custom-call(s32[192,11]{1,0:T(8,128)} %copy.6.ids_hbm, bf16[1,768,2048]{2,1,0:T(8,128)(2,1)} %q_hbm.1, bf16[1,12,64,2048]{3,2,1,0:T(8,128)(2,1)} %bitcast.2, bf16[1,12,64,2048]{3,2,1,0:T(8,128)(2,1)} %bitcast.3, bf16[2048,4096]{1,0:T(8,128)(2,1)} %w_hbm.1), custom_call_target="tpu_custom_call" | custom-call | flops 11000000512 | bytes 20971520 | tf_op jit(solution)/shard_map/pallas_call | solution.py:264
  134.6 1.7 %copy.8 = bf16[768,2048]{1,0:T(8,128)(2,1)} copy(bf16[768,2048]{1,0:T(8,128)(2,1)S(1)} %shard_map.55) | data formatting | bytes 6291456

commit v3 on v2

--- a/solution.py
+++ b/solution.py
@@ -19,6 +19,7 @@
 ROUNDS = 6
 TILES = ROWS // TILE
 BLK = 2
+STORES = 4
 PAIR = 2 * TILE
 PAIRS = ROUNDS * SEQ
 SPAN = NB * TILE
@@ -34,8 +35,8 @@
 
 
 def kernel(
-    ids_hbm, q_hbm, k_hbm, v_hbm, w_hbm, out_hbm,
-    q_buf, k_buf, v_buf, w_buf, att, swapped, folded, gathered,
+    ids_hbm, q_hbm, k_hbm, v_hbm, w_hbm, out_ref, last_ref, w_buf,
+    q_buf, k_buf, v_buf, att, swapped, folded, gathered,
     s_even, s_odd, p_even, p_odd,
     ids, ids_sem, w_sem, k_send, k_recv, v_send, v_recv, q_send, q_recv,
     x_send, x_recv, g_send, g_recv, f_send, f_recv,
@@ -113,7 +114,7 @@
     ids_copy.wait()
 
     def near(buf, tile):
-        return jnp.concatenate([buf[ids[tile, j]] for j in range(NB)], axis=0)
+        return jnp.concatenate([buf[ids[j, tile]] for j in range(NB)], axis=0)
 
     def near_pair(buf, pair):
         tile = (pair % SEQ) * TILES + (pair // SEQ) * 2
@@ -215,7 +216,7 @@
 
         def columns(n, _):
             cols = pl.ds(pl.multiple_of(n * 512, 512), 512)
-            out_hbm[rows, cols] = jnp.dot(
+            out_ref[rows, cols] = jnp.dot(
                 gathered[rows, :], w_buf[:, cols], preferred_element_type=jnp.float32
             ).astype(jnp.bfloat16)
             return 0
@@ -244,12 +245,35 @@
         return 0
 
     lax.fori_loop(0, last, finish, 0)
-    project(last)
+    await_bytes(gathered.at[round_rows(last, 1 - core)], f_recv.at[last])
+    last_ref[...] = gathered[pl.ds(last * PAIR, PAIR), :]
 
     await_bytes(q_buf.at[:, pl.ds(0, SEQ - 1)], q_send)
     await_bytes(swapped, x_send)
     await_bytes(folded.at[:, pl.ds(0, SEQ - 1)], g_send)
     await_bytes(swapped, f_send)
+
+
+def finish_kernel(done, last_rows, w_half, out_hbm, last_out, sems, last_sem):
+    size = done.shape[0] // STORES
+    stores = [
+        pltpu.make_async_copy(
+            done.at[pl.ds(n * size, size)], out_hbm.at[pl.ds(n * size, size)], sems.at[n]
+        )
+        for n in range(STORES)
+    ]
+    for store in stores:
+        store.start()
+    step = 512
+    for n in range(last_out.shape[1] // step):
+        cols = pl.ds(n * step, step)
+        last_out[:, cols] = jnp.dot(
+            last_rows[...], w_half[:, cols], preferred_element_type=jnp.float32
+        ).astype(jnp.bfloat16)
+    store = pltpu.make_async_copy(last_out, out_hbm.at[pl.ds(done.shape[0], PAIR)], last_sem)
+    store.start()
+    for each in (*stores, store):
+        each.wait()
 
 
 def by_tile(tokens):
@@ -261,16 +285,19 @@
     dma = pltpu.SemaphoreType.DMA
     vmem = pltpu.VMEM
     width = w_out.shape[1] // 2
-    return pl.pallas_call(
+    done, last_rows, w_half = pl.pallas_call(
         kernel,
-        out_shape=pltpu.VMEM((ROWS, width), bf16),
+        out_shape=(
+            vmem((ROWS - PAIR, width), bf16),
+            vmem((PAIR, HEADS * HD), bf16),
+            vmem((HEADS * HD, width), bf16),
+        ),
         in_specs=[pl.BlockSpec(memory_space=pl.ANY)] * 5,
-        out_specs=pl.BlockSpec(memory_space=pltpu.VMEM),
+        out_specs=[pl.BlockSpec(memory_space=vmem)] * 3,
         scratch_shapes=[
             vmem((ROUNDS, SEQ, PAIR, HD), bf16),
             vmem((SEQ * TILES, TILE, HD), bf16),
             vmem((SEQ * TILES, TILE, HD), bf16),
-            vmem((HEADS * HD, width), bf16),
             vmem((ROUNDS, 2, SEQ, TILE, HD), bf16),
             vmem((ROUNDS, SEQ, TILE, HD), bf16),
             vmem((ROUNDS, SEQ, TILE, HD), bf16),
@@ -279,7 +306,7 @@
             vmem((SPAN, PAIR), f32),
             vmem((SPAN, PAIR), bf16),
             vmem((SPAN, PAIR), bf16),
-            pltpu.SMEM((SEQ * TILES, NB), jnp.int32), dma, dma,
+            pltpu.SMEM((NB, SEQ * TILES), jnp.int32), dma, dma,
             dma, dma, dma, dma,
             dma, dma((ROUNDS,)),
             dma, dma((ROUNDS,)),
@@ -287,12 +314,20 @@
             dma, dma((ROUNDS,)),
         ],
         compiler_params=pltpu.CompilerParams(
-            collective_id=0, has_side_effects=True, vmem_limit_bytes=56 * 2**20
+            collective_id=0, has_side_effects=True, vmem_limit_bytes=50 * 2**20
         ),
         cost_estimate=pl.CostEstimate(
             flops=11_000_000_000, bytes_accessed=20 * 2**20, transcendentals=8_700_000
         ),
-    )(neighbours, queries, by_tile(keys), by_tile(values), w_out)
+    )(neighbours.T, queries, by_tile(keys), by_tile(values), w_out)
+    return pl.pallas_call(
+        finish_kernel,
+        out_shape=jax.ShapeDtypeStruct((ROWS, width), bf16),
+        in_specs=[pl.BlockSpec(memory_space=vmem)] * 3,
+        out_specs=pl.BlockSpec(memory_space=pl.ANY),
+        scratch_shapes=[vmem((PAIR, width), bf16), dma((STORES,)), dma],
+        compiler_params=pltpu.CompilerParams(vmem_limit_bytes=40 * 2**20),
+    )(done, last_rows, w_half)
 
 
 def solution(mesh):

time: 136 us -> 134 us (0.985)
  local copies, waits for them, and re-layouts: 3.13 us -> 0 us
    unnamed x2 -> x0, local copies, waits for them, and re-layouts: 3.13 us -> none
    pallas_call x1 -> x2, Pallas kernels: 133 us -> 134 us  [the longest x1 132 us: on_device(): pl.pallas_call(kernel, out_shape=(vmem((ROWS - PAIR, width), bf16), vmem(...]
where the time goes in v3:
time: 134 us
  Pallas kernels  134 us (100%)
    pallas_call x1, Pallas kernels, on_device(): pl.pallas_call(kernel, out_shape=(vmem((ROWS - PAIR, width), bf16), vmem(...  132 us

profile of v3, /device:TPU:1, one launch (start us, length us, event | category | flops | bytes accessed | tf_op | source)
XLA Modules:
  0.0 133.6 jit_solution(16027230421087015740)
XLA Ops:
  0.0 131.5 %shard_map.55 = (bf16[640,2048]{1,0:T(8,128)(2,1)S(1)}, bf16[128,2048]{1,0:T(8,128)(2,1)S(1)}, bf16[2048,2048]{1,0:T(8,128)(2,1)S(1)}) custom-call(s32[11,192]{1,0:T(8,128)} %bitcast.5, bf16[1,768,2048]{2,1,0:T(8,128)(2,1)} %q_hbm.1, bf16[1,12,64,2048]{3,2,1,0:T(8,128)(2,1)} %bitcast.3, bf16[1,12,64,2048]{3,2,1,0:T(8,128)(2,1)} %bitcast.4, ...), custom_call_target="tpu_custom_call" | custom-call | flops 11000000512 | bytes 20971520 | tf_op jit(solution)/shard_map/pallas_call | solution.py:288
  131.5 2.1 %shard_map.56 = bf16[768,2048]{1,0:T(8,128)(2,1)} custom-call(bf16[640,2048]{1,0:T(8,128)(2,1)S(1)} %get-tuple-element.8.done, bf16[128,2048]{1,0:T(8,128)(2,1)S(1)} %get-tuple-element.9.last_rows, bf16[2048,2048]{1,0:T(8,128)(2,1)S(1)} %get-tuple-element.10.w_half), custom_call_target="tpu_custom_call" | custom-call | tf_op jit(solution)/shard_map/pallas_call | solution.py:323

commit v4 on v3

--- a/solution.py
+++ b/solution.py
@@ -18,8 +18,14 @@
 ROWS = 768
 ROUNDS = 6
 TILES = ROWS // TILE
+MIXED = (
+    (1, 2), (3, 0), (0, 1), (2, 3), (3, 2), (1, 0), (0, 3), (2, 1),
+    (2, 2), (1, 1), (3, 3), (0, 2), (2, 0), (1, 3), (3, 1),
+)
 BLK = 2
+NEAR = 9
 STORES = 4
+COLS = 512
 PAIR = 2 * TILE
 PAIRS = ROUNDS * SEQ
 SPAN = NB * TILE
@@ -50,6 +56,8 @@
     def await_bytes(ref, sem):
         pltpu.make_async_copy(ref, ref, sem).wait()
 
+    mixed = [lax.rem(z + dz, RING) * RING + lax.rem(y + dy, RING) for dz, dy in MIXED]
+
     barrier = pltpu.get_barrier_semaphore()
     for peer in peers:
         pl.semaphore_signal(barrier, inc=1, device_id={"seq": peer}, device_id_type=MESH)
@@ -63,7 +71,7 @@
         tiles = pl.ds(me * TILES, TILES)
 
         def block(n, _):
-            for peer in peers:
+            for peer in mixed:
                 pltpu.make_async_remote_copy(
                     src_ref=src.at[0, pl.ds(n * BLK, BLK), :, head_cols(peer)],
                     dst_ref=buf.at[pl.ds(me * TILES + n * BLK, BLK)],
@@ -77,20 +85,23 @@
         lax.fori_loop(0, TILES // BLK, block, 0)
         pltpu.make_async_copy(src.at[0, :, :, head_cols(me)], buf.at[tiles], recv).start()
 
-    def scatter_queries(r, _):
+    def scatter_queries(r, recv_of):
         rows = pl.ds(pl.multiple_of(r * PAIR, PAIR), PAIR)
-        for peer in peers:
+        for n, peer in enumerate(peers):
             pltpu.make_async_remote_copy(
                 src_ref=q_hbm.at[0, rows, head_cols(peer)],
                 dst_ref=q_buf.at[r, me],
                 send_sem=q_send,
-                recv_sem=q_recv.at[r],
+                recv_sem=recv_of(n),
                 device_id={"seq": peer},
                 device_id_type=MESH,
             ).start()
         pltpu.make_async_copy(
-            q_hbm.at[0, rows, head_cols(me)], q_buf.at[r, me], q_recv.at[r]
+            q_hbm.at[0, rows, head_cols(me)], q_buf.at[r, me], recv_of(0)
         ).start()
+
+    def scatter_later_queries(r, _):
+        scatter_queries(r, lambda _: q_recv.at[r + 1])
         return 0
 
     remote_tiles = pl.ds(0, (SEQ - 1) * TILES)
@@ -105,7 +116,8 @@
     for ref in (s_even, s_odd, p_even, p_odd):
         ref[...] = jnp.zeros_like(ref)
     scatter(v_hbm, v_buf, v_send, v_recv)
-    lax.fori_loop(0, ROUNDS, scatter_queries, 0)
+    scatter_queries(0, lambda n: q_recv.at[n // (NEAR - 1)])
+    lax.fori_loop(1, ROUNDS, scatter_later_queries, 0)
     await_bytes(k_buf.at[remote_tiles], k_send)
     await_bytes(v_buf.at[remote_tiles], v_send)
     await_bytes(k_buf, k_recv)
@@ -116,8 +128,17 @@
     def near(buf, tile):
         return jnp.concatenate([buf[ids[j, tile]] for j in range(NB)], axis=0)
 
+    def source(pair):
+        n = pair % SEQ
+        far = n // NEAR
+        k = n - NEAR
+        side = jnp.maximum(k, 0) // RING
+        dz = (1 - far) * (n // 3 - 1) + far * ((1 - side) * 2 + side * (k - RING - 1))
+        dy = (1 - far) * (n % 3 - 1) + far * ((1 - side) * k + side * 2)
+        return (z + dz + RING) % RING * RING + (y + dy + RING) % RING
+
     def near_pair(buf, pair):
-        tile = (pair % SEQ) * TILES + (pair // SEQ) * 2
+        tile = source(pair) * TILES + (pair // SEQ) * 2
         return jnp.concatenate([near(buf, tile), near(buf, tile + 1)], axis=1)
 
     def step(i, scores_in, scores_out, probs_in, probs_out):
@@ -126,15 +147,15 @@
             probs_in[...], near_pair(v_buf, done), (((0,), (0,)), ((), ())),
             preferred_element_type=jnp.float32,
         )
-        att[done // SEQ, 0, done % SEQ] = result[:TILE, :HD].astype(jnp.bfloat16)
-        att[done // SEQ, 1, done % SEQ] = result[TILE:, HD:].astype(jnp.bfloat16)
+        att[done // SEQ, 0, source(done)] = result[:TILE, :HD].astype(jnp.bfloat16)
+        att[done // SEQ, 1, source(done)] = result[TILE:, HD:].astype(jnp.bfloat16)
         scores = scores_in[...]
         peak = jnp.max(scores, axis=0, keepdims=True) * EXP_SCALE
         expval = jnp.exp2(scores * EXP_SCALE - peak)
         total = jnp.sum(expval, axis=0, keepdims=True)
         probs_out[...] = (expval * (1.0 / total)).astype(jnp.bfloat16)
         pair = jnp.minimum(i, PAIRS - 1)
-        queries = q_buf[pair // SEQ, pair % SEQ]
+        queries = q_buf[pair // SEQ, source(pair)]
         zero = jnp.zeros((TILE, HD), jnp.bfloat16)
         blocks = jnp.concatenate(
             [
@@ -210,42 +231,56 @@
             device_id_type=MESH,
         ).start()
 
-    def project(r):
-        await_bytes(gathered.at[round_rows(r, 1 - core)], f_recv.at[r])
-        rows = pl.ds(pl.multiple_of(r * PAIR, PAIR), PAIR)
+    def project(r, rounds, first, count):
+        rows = pl.ds(pl.multiple_of(r * PAIR, PAIR), rounds * PAIR)
 
         def columns(n, _):
-            cols = pl.ds(pl.multiple_of(n * 512, 512), 512)
+            cols = pl.ds(pl.multiple_of(n * COLS, COLS), COLS)
             out_ref[rows, cols] = jnp.dot(
                 gathered[rows, :], w_buf[:, cols], preferred_element_type=jnp.float32
             ).astype(jnp.bfloat16)
             return 0
 
-        lax.fori_loop(0, half_cols // 512, columns, 0)
+        lax.fori_loop(first, first + count, columns, 0)
+
+    def await_forward(r):
+        await_bytes(gathered.at[round_rows(r, 1 - core)], f_recv.at[r])
 
     def one_round(r, _):
-        await_bytes(q_buf.at[r], q_recv.at[r])
+        await_bytes(q_buf.at[r], q_recv.at[r + 1])
         steps(r * SEQ, 2)
-        pl.when(r >= 1)(lambda: swap(r - 1).start())
+        swap(r - 1).start()
         steps(r * SEQ + 2, 8)
-        pl.when(r >= 1)(lambda: fold(r - 1))
+        fold(r - 1)
         steps(r * SEQ + 10, 6)
         return 0
 
-    lax.fori_loop(0, ROUNDS, one_round, 0)
+    await_bytes(q_buf.at[0, pl.ds(0, NEAR)], q_recv.at[0])
+    steps(0, NEAR - 1)
+    await_bytes(q_buf.at[0, pl.ds(0, SEQ - NEAR)], q_recv.at[1])
+    steps(NEAR - 1, SEQ - NEAR + 1)
+    lax.fori_loop(1, ROUNDS, one_round, 0)
     steps(PAIRS, 2)
     last = ROUNDS - 1
     swap(last).start()
     fold(last)
+    blocks = half_cols // COLS
     forward(0)
-
-    def finish(r, _):
-        forward(r + 1)
-        project(r)
-        return 0
-
-    lax.fori_loop(0, last, finish, 0)
-    await_bytes(gathered.at[round_rows(last, 1 - core)], f_recv.at[last])
+    forward(1)
+    forward(2)
+    await_forward(0)
+    await_forward(1)
+    project(0, 2, 0, 4)
+    forward(3)
+    await_forward(2)
+    project(2, 1, 0, 4)
+    forward(4)
+    await_forward(3)
+    project(3, 1, 0, 4)
+    forward(5)
+    await_forward(4)
+    project(4, 1, 0, 4)
+    await_forward(5)
     last_ref[...] = gathered[pl.ds(last * PAIR, PAIR), :]
 
     await_bytes(q_buf.at[:, pl.ds(0, SEQ - 1)], q_send)
@@ -308,7 +343,7 @@
             vmem((SPAN, PAIR), bf16),
             pltpu.SMEM((NB, SEQ * TILES), jnp.int32), dma, dma,
             dma, dma, dma, dma,
-            dma, dma((ROUNDS,)),
+            dma, dma((ROUNDS + 1,)),
             dma, dma((ROUNDS,)),
             dma, dma((ROUNDS,)),
             dma, dma((ROUNDS,)),

time: 134 us -> 133 us (level)
  no operation moved by 1% of the time
where the time goes in v4:
time: 133 us
  Pallas kernels  133 us (100%)
    pallas_call x1, Pallas kernels, on_device(): pl.pallas_call(kernel, out_shape=(vmem((ROWS - PAIR, width), bf16), vmem(...  131 us

profile of v4, /device:TPU:1, one launch (start us, length us, event | category | flops | bytes accessed | tf_op | source)
XLA Modules:
  0.0 132.7 jit_solution(7036097234849849099)
XLA Ops:
  0.0 130.6 %shard_map.55 = (bf16[640,2048]{1,0:T(8,128)(2,1)S(1)}, bf16[128,2048]{1,0:T(8,128)(2,1)S(1)}, bf16[2048,2048]{1,0:T(8,128)(2,1)S(1)}) custom-call(s32[11,192]{1,0:T(8,128)} %bitcast.5, bf16[1,768,2048]{2,1,0:T(8,128)(2,1)} %q_hbm.1, bf16[1,12,64,2048]{3,2,1,0:T(8,128)(2,1)} %bitcast.3, bf16[1,12,64,2048]{3,2,1,0:T(8,128)(2,1)} %bitcast.4, ...), custom_call_target="tpu_custom_call" | custom-call | flops 11000000512 | bytes 20971520 | tf_op jit(solution)/shard_map/pallas_call | solution.py:323
  130.6 2.1 %shard_map.56 = bf16[768,2048]{1,0:T(8,128)(2,1)} custom-call(bf16[640,2048]{1,0:T(8,128)(2,1)S(1)} %get-tuple-element.8.done, bf16[128,2048]{1,0:T(8,128)(2,1)S(1)} %get-tuple-element.9.last_rows, bf16[2048,2048]{1,0:T(8,128)(2,1)S(1)} %get-tuple-element.10.w_half), custom_call_target="tpu_custom_call" | custom-call | tf_op jit(solution)/shard_map/pallas_call | solution.py:358

commit v5 on v4

--- a/solution.py
+++ b/solution.py
@@ -263,10 +263,10 @@
     steps(PAIRS, 2)
     last = ROUNDS - 1
     swap(last).start()
+    forward(0)
+    forward(1)
     fold(last)
     blocks = half_cols // COLS
-    forward(0)
-    forward(1)
     forward(2)
     await_forward(0)
     await_forward(1)

time: 133 us -> 133 us (level)
  no operation moved by 1% of the time
where the time goes in v5:
time: 133 us; the launch traced here: 132 us
  Pallas kernels  132 us (99%)
    pallas_call x1, Pallas kernels, on_device(): pl.pallas_call(kernel, out_shape=(vmem((ROWS - PAIR, width), bf16), vmem(...  130 us

profile of v5, /device:TPU:1, one launch (start us, length us, event | category | flops | bytes accessed | tf_op | source)
XLA Modules:
  0.0 132.4 jit_solution(11968524024581829371)
XLA Ops:
  0.0 130.3 %shard_map.55 = (bf16[640,2048]{1,0:T(8,128)(2,1)S(1)}, bf16[128,2048]{1,0:T(8,128)(2,1)S(1)}, bf16[2048,2048]{1,0:T(8,128)(2,1)S(1)}) custom-call(s32[11,192]{1,0:T(8,128)} %bitcast.5, bf16[1,768,2048]{2,1,0:T(8,128)(2,1)} %q_hbm.1, bf16[1,12,64,2048]{3,2,1,0:T(8,128)(2,1)} %bitcast.3, bf16[1,12,64,2048]{3,2,1,0:T(8,128)(2,1)} %bitcast.4, ...), custom_call_target="tpu_custom_call" | custom-call | flops 11000000512 | bytes 20971520 | tf_op jit(solution)/shard_map/pallas_call | solution.py:323
  130.3 2.1 %shard_map.56 = bf16[768,2048]{1,0:T(8,128)(2,1)} custom-call(bf16[640,2048]{1,0:T(8,128)(2,1)S(1)} %get-tuple-element.8.done, bf16[128,2048]{1,0:T(8,128)(2,1)S(1)} %get-tuple-element.9.last_rows, bf16[2048,2048]{1,0:T(8,128)(2,1)S(1)} %get-tuple-element.10.w_half), custom_call_target="tpu_custom_call" | custom-call | tf_op jit(solution)/shard_map/pallas_call | solution.py:358

commit v6 on v5

--- a/solution.py
+++ b/solution.py
@@ -141,7 +141,7 @@
         tile = source(pair) * TILES + (pair // SEQ) * 2
         return jnp.concatenate([near(buf, tile), near(buf, tile + 1)], axis=1)
 
-    def step(i, scores_in, scores_out, probs_in, probs_out):
+    def step(i, scores_in, scores_out, probs_in, probs_out, left=3):
         done = jnp.maximum(i - 2, 0)
         result = lax.dot_general(
             probs_in[...], near_pair(v_buf, done), (((0,), (0,)), ((), ())),
@@ -149,11 +149,15 @@
         )
         att[done // SEQ, 0, source(done)] = result[:TILE, :HD].astype(jnp.bfloat16)
         att[done // SEQ, 1, source(done)] = result[TILE:, HD:].astype(jnp.bfloat16)
+        if left == 1:
+            return
         scores = scores_in[...]
         peak = jnp.max(scores, axis=0, keepdims=True) * EXP_SCALE
         expval = jnp.exp2(scores * EXP_SCALE - peak)
         total = jnp.sum(expval, axis=0, keepdims=True)
         probs_out[...] = (expval * (1.0 / total)).astype(jnp.bfloat16)
+        if left == 2:
+            return
         pair = jnp.minimum(i, PAIRS - 1)
         queries = q_buf[pair // SEQ, source(pair)]
         zero = jnp.zeros((TILE, HD), jnp.bfloat16)
@@ -260,7 +264,8 @@
     await_bytes(q_buf.at[0, pl.ds(0, SEQ - NEAR)], q_recv.at[1])
     steps(NEAR - 1, SEQ - NEAR + 1)
     lax.fori_loop(1, ROUNDS, one_round, 0)
-    steps(PAIRS, 2)
+    step(PAIRS, s_odd, s_even, p_even, p_odd, 2)
+    step(PAIRS + 1, s_even, s_odd, p_odd, p_even, 1)
     last = ROUNDS - 1
     swap(last).start()
     forward(0)

time: 133 us -> 133 us (level)
  no operation moved by 1% of the time
where the time goes in v6:
time: 133 us
  Pallas kernels  133 us (100%)
    pallas_call x1, Pallas kernels, on_device(): pl.pallas_call(kernel, out_shape=(vmem((ROWS - PAIR, width), bf16), vmem(...  130 us

profile of v6, /device:TPU:1, one launch (start us, length us, event | category | flops | bytes accessed | tf_op | source)
XLA Modules:
  0.0 132.5 jit_solution(7352395631036211439)
XLA Ops:
  0.0 130.4 %shard_map.55 = (bf16[640,2048]{1,0:T(8,128)(2,1)S(1)}, bf16[128,2048]{1,0:T(8,128)(2,1)S(1)}, bf16[2048,2048]{1,0:T(8,128)(2,1)S(1)}) custom-call(s32[11,192]{1,0:T(8,128)} %bitcast.5, bf16[1,768,2048]{2,1,0:T(8,128)(2,1)} %q_hbm.1, bf16[1,12,64,2048]{3,2,1,0:T(8,128)(2,1)} %bitcast.3, bf16[1,12,64,2048]{3,2,1,0:T(8,128)(2,1)} %bitcast.4, ...), custom_call_target="tpu_custom_call" | custom-call | flops 11000000512 | bytes 20971520 | tf_op jit(solution)/shard_map/pallas_call | solution.py:328
  130.4 2.1 %shard_map.56 = bf16[768,2048]{1,0:T(8,128)(2,1)} custom-call(bf16[640,2048]{1,0:T(8,128)(2,1)S(1)} %get-tuple-element.8.done, bf16[128,2048]{1,0:T(8,128)(2,1)S(1)} %get-tuple-element.9.last_rows, bf16[2048,2048]{1,0:T(8,128)(2,1)S(1)} %get-tuple-element.10.w_half), custom_call_target="tpu_custom_call" | custom-call | tf_op jit(solution)/shard_map/pallas_call | solution.py:363

commit v7 on v5

--- a/solution.py
+++ b/solution.py
@@ -22,7 +22,7 @@
     (1, 2), (3, 0), (0, 1), (2, 3), (3, 2), (1, 0), (0, 3), (2, 1),
     (2, 2), (1, 1), (3, 3), (0, 2), (2, 0), (1, 3), (3, 1),
 )
-BLK = 2
+BLK = 1
 NEAR = 9
 STORES = 4
 COLS = 512

time: 133 us -> 133 us (level)
  no operation moved by 1% of the time
where the time goes in v7:
time: 133 us; the launch traced here: 132 us
  Pallas kernels  132 us (99%)
    pallas_call x1, Pallas kernels, on_device(): pl.pallas_call(kernel, out_shape=(vmem((ROWS - PAIR, width), bf16), vmem(...  130 us

profile of v7, /device:TPU:1, one launch (start us, length us, event | category | flops | bytes accessed | tf_op | source)
XLA Modules:
  0.0 132.4 jit_solution(5428816133335546101)
XLA Ops:
  0.0 130.3 %shard_map.55 = (bf16[640,2048]{1,0:T(8,128)(2,1)S(1)}, bf16[128,2048]{1,0:T(8,128)(2,1)S(1)}, bf16[2048,2048]{1,0:T(8,128)(2,1)S(1)}) custom-call(s32[11,192]{1,0:T(8,128)} %bitcast.5, bf16[1,768,2048]{2,1,0:T(8,128)(2,1)} %q_hbm.1, bf16[1,12,64,2048]{3,2,1,0:T(8,128)(2,1)} %bitcast.3, bf16[1,12,64,2048]{3,2,1,0:T(8,128)(2,1)} %bitcast.4, ...), custom_call_target="tpu_custom_call" | custom-call | flops 11000000512 | bytes 20971520 | tf_op jit(solution)/shard_map/pallas_call | solution.py:323
  130.3 2.1 %shard_map.56 = bf16[768,2048]{1,0:T(8,128)(2,1)} custom-call(bf16[640,2048]{1,0:T(8,128)(2,1)S(1)} %get-tuple-element.8.done, bf16[128,2048]{1,0:T(8,128)(2,1)S(1)} %get-tuple-element.9.last_rows, bf16[2048,2048]{1,0:T(8,128)(2,1)S(1)} %get-tuple-element.10.w_half), custom_call_target="tpu_custom_call" | custom-call | tf_op jit(solution)/shard_map/pallas_call | solution.py:358
